TPU v7x, 32 devices: a whole 2x2x4 slice. The times are simulated.
32 devices in a mesh: occ: 4 (over y, core), vir: 8 (over z, x).
Axes of the slice: x: 2, y: 2, z: 4, core: 2. Of those that a mesh axis runs over, the one named last changes fastest.
Arguments:
- orbitals: bfloat16 [4, 2048, 4096], P('occ', 'vir'), may hold values from -0.75 to 0.75
- eps_occ: bfloat16 [4], P('occ'), may hold values from -2.5 to -0.5
- eps_vir: bfloat16 [2048], P('vir'), may hold values from 0.5 to 3
Outputs:
- density: bfloat16 [4, 2048, 4096], P('occ', 'vir')
All inputs are finite; a program needn't handle non-finite values.
Results may differ from a plain program's by a relative error of at most 0.0047.
Values may be sent and summed in bfloat16 or wider, within the bound.
A program may use at most 64 MiB of HBM per device.

v0:
```python
import jax
import jax.numpy as jnp
from jax import lax
from jax.sharding import PartitionSpec as P

BATCH_DEV = 8
REACH = 1


def shifted_2(block, axis, distance):
    devices = range(lax.axis_size(axis))
    route = [((i - distance) % len(devices), i) for i in devices]
    return lax.ppermute(block, axis, route)


def pair_energies(eps_occ, occ_stack, eps_vir, batch_energy):
    own_energy = eps_occ.astype(jnp.float32)
    others = occ_stack.astype(jnp.float32)
    vir_energy = eps_vir.astype(jnp.float32)
    batch_virt = batch_energy.astype(jnp.float32)
    return (
        vir_energy[None, :, None, None, None]
        + batch_virt[None, None, None, None, :]
        - own_energy[:, None, None, None, None]
        - others[None, None, :, :, None]
    )


def shards(orbitals, eps_occ, eps_vir):
    occ_dev, vir_dev, aux_width = orbitals.shape
    block_count = 2 * REACH + 1
    offsets = list(range(-REACH, REACH + 1))
    own_rows = orbitals[:, :BATCH_DEV, :]
    resident = orbitals.reshape(occ_dev * vir_dev, aux_width)
    energies = []
    row_blocks = []
    for offset in offsets:
        if offset == 0:
            row_blocks.append(own_rows)
            energies.append(eps_occ)
        else:
            shifted, shifted_energy = shifted_2((own_rows, eps_occ), "occ", -offset)
            row_blocks.append(shifted)
            energies.append(shifted_energy)
    stacked = jnp.stack(row_blocks)
    row_sets, batch_energy = (
        lax.all_gather(stacked, "vir", axis=2, tiled=True),
        lax.all_gather(eps_vir[:BATCH_DEV], "vir", axis=0, tiled=True),
    )
    batch_width = row_sets.shape[2]
    coulomb = jnp.einsum(
        "rp,cp->rc",
        resident,
        row_sets.reshape(block_count * occ_dev * batch_width, aux_width),
        preferred_element_type=jnp.float32,
    )
    coulomb = coulomb.reshape(occ_dev, vir_dev, block_count, occ_dev, batch_width)
    mirrors = []
    for position, offset in enumerate(offsets):
        mirror = coulomb[:, :, block_count - 1 - position]
        if offset != 0:
            mirror = shifted_2(mirror, "occ", -offset)
        mirrors.append(jnp.transpose(mirror, (2, 1, 0, 3)))
    exchange = jnp.stack(mirrors, axis=2)
    denominator = pair_energies(eps_occ, jnp.stack(energies), eps_vir, batch_energy)
    amplitude = ((2.0 * coulomb - exchange) / denominator).astype(jnp.bfloat16)
    density = jnp.dot(
        amplitude.reshape(occ_dev * vir_dev, block_count * occ_dev * batch_width),
        row_sets.reshape(block_count * occ_dev * batch_width, aux_width),
        preferred_element_type=jnp.float32,
    )
    return density.reshape(occ_dev, vir_dev, aux_width).astype(jnp.bfloat16)


def solution(mesh):
    return jax.shard_map(
        shards,
        mesh=mesh,
        in_specs=(P("occ", "vir", None), P("occ"), P("vir")),
        out_specs=P("occ", "vir", None),
        check_vma=False,
    )
```

profile of v0, /device:TPU:0, one launch (start us, length us, event | category | flops | bytes accessed | tf_op | source)
XLA Modules:
  0.0 76.2 jit_solution(13789884879793890402)
XLA Ops:
  6.5 0.0 all-gather.2.cloned.1.call-start
  6.5 0.8 %slice_bitcast_fusion.2 = (bf16[1,1,8,4096]{3,2,1,0:T(8,128)(2,1)S(1)}, bf16[1,8,4096]{2,1,0:T(8,128)(2,1)S(1)}) fusion(bf16[1,256,4096]{2,1,0:T(8,128)(2,1)} %param.3), kind=kLoop, calls=%fused_computation.16 | loop fusion | bytes 196608 | tf_op jit(solution)/shard_map/stack | solution.py:45
  7.4 2.5 %collective-permute-start.1 = (bf16[1,8,4096]{2,1,0:T(8,128)(2,1)S(1)}, bf16[1,8,4096]{2,1,0:T(8,128)(2,1)S(1)}, u32[]{:S(2)}, u32[]{:S(2)}) collective-permute-start(bf16[1,8,4096]{2,1,0:T(8,128)(2,1)S(1)} %get-tuple-element.6), channel_id=1, source_target_pairs={{8,0},{16,8},{24,16},{0,24},{9,1},{17,9},{25,17},{1,25},{10,2},{18... | collective-permute-start | bytes 196616 | tf_op jit(solution)/shard_map/ppermute | solution.py:13
  9.8 0.0 collective-permute-start
  9.9 2.4 %collective-permute-done.1 = bf16[1,8,4096]{2,1,0:T(8,128)(2,1)S(1)} collective-permute-done((bf16[1,8,4096]{2,1,0:T(8,128)(2,1)S(1)}, bf16[1,8,4096]{2,1,0:T(8,128)(2,1)S(1)}, u32[]{:S(2)}, u32[]{:S(2)}) %collective-permute-start.1) | collective-permute-done | bytes 65568 | tf_op jit(solution)/shard_map/ppermute | solution.py:13
  12.3 1.3 %collective-permute-done = bf16[1,8,4096]{2,1,0:T(8,128)(2,1)S(1)} collective-permute-done((bf16[1,8,4096]{2,1,0:T(8,128)(2,1)S(1)}, bf16[1,8,4096]{2,1,0:T(8,128)(2,1)S(1)}, u32[]{:S(2)}, u32[]{:S(2)}) %collective-permute-start) | collective-permute-done | bytes 65568 | tf_op jit(solution)/shard_map/ppermute | solution.py:13
  13.5 0.7 pad_maximum_fusion
  14.2 0.0 all-gather.2.cloned.1.call-update
  14.3 0.1 collective-permute-start.4
  14.3 1.7 %collective-permute-start.5 = (bf16[1]{0:T(256)(128)(2,1)}, bf16[1]{0:T(256)(128)(2,1)}, u32[]{:S(2)}, u32[]{:S(2)}) collective-permute-start(bf16[1]{0:T(256)(128)(2,1)} %param.4), channel_id=1, source_target_pairs={{8,0},{16,8},{24,16},{0,24},{9,1},{17,9},{25,17},{1,25},{10,2},{18... | collective-permute-start | bytes 14 | tf_op jit(solution)/shard_map/ppermute | solution.py:13
  16.8 0.7 convert_element_type.28
  17.4 1.3 %dynamic-slice = u32[1]{0:T(128)} dynamic-slice(u32[32]{0:T(128)} %constant.6, u32[]{:T(128)S(6)} %add.21), dynamic_slice_sizes={1} | dynamic-slice | bytes 12
  19.4 0.9 %dynamic-update-slice = bf16[64]{0:T(256)(128)(2,1)S(1)} dynamic-update-slice(bf16[64]{0:T(256)(128)(2,1)S(1)} %broadcast.40, bf16[8]{0:T(256)(128)(2,1)} %bitcast.51, u32[]{:T(128)} %bitcast.15) | dynamic-update-slice | bytes 36
  20.3 21.7 %all-reduce = bf16[64]{0:T(256)(128)(2,1)S(1)} all-reduce(bf16[64]{0:T(256)(128)(2,1)S(1)} %dynamic-update-slice), channel_id=1, replica_groups=mesh['occ'=4,'vir'=8] {'vir'}, use_global_device_ids=true, to_apply=%add | all-reduce | flops 64 | bytes 256
  41.9 0.1 add_subtract_fusion
  42.0 0.0 collective-permute-done.4
  42.0 0.0 collective-permute-done.5
  42.0 1.4 %maximum_convert_fusion = f32[3]{0:T(128)S(1)} fusion(bf16[1]{0:T(256)(128)(2,1)} %collective-permute-done.5, bf16[1]{0:T(256)(128)(2,1)} %copy.7, bf16[1]{0:T(256)(128)(2,1)} %collective-permute-done.4), kind=kLoop, calls=%fused_computation.15 | loop fusion | flops 18 | bytes 18 | tf_op jit(solution)/shard_map/convert_element_type | solution.py:18
  43.4 16.2 %all-gather.2.cloned.1.call-done = bf16[3,1,64,4096]{3,2,1,0:T(8,128)(2,1)} async-done(((bf16[3,1,8,4096]{3,2,1,0:T(8,128)(2,1)}), bf16[3,1,64,4096]{3,2,1,0:T(8,128)(2,1)}) %all-gather.2.cloned.1.call-update) | async-done | bytes 1572880 | tf_op jit(solution)/shard_map/all_gather | solution.py:47
  59.7 0.0 copy-start
  59.7 3.0 %fusion.1 = f32[192,256]{1,0:T(8,128)S(1)} fusion(bf16[192,4096]{1,0:T(8,128)(2,1)} %bitcast.43, bf16[1,256,4096]{2,1,0:T(8,128)(2,1)} %param.3), kind=kOutput, calls=%fused_computation.2 | convolution fusion | flops 402653184 | bytes 3866624 | tf_op jit(solution)/shard_map/rp,cp->rc/dot_general | solution.py:51
  62.7 0.3 collective-permute-start.3
  63.1 0.3 collective-permute-start.2
  63.4 0.1 broadcast_reduce_fusion
  63.4 0.1 sub.53
  63.5 1.5 %collective-permute-done.3 = f32[1,256,1,64]{1,3,2,0:T(8,128)S(1)} collective-permute-done((f32[1,256,1,64]{1,3,2,0:T(8,128)S(1)}, f32[1,256,1,64]{1,3,2,0:T(8,128)S(1)}, u32[]{:S(2)}, u32[]{:S(2)}) %collective-permute-start.3) | collective-permute-done | bytes 65568 | tf_op jit(solution)/shard_map/ppermute | solution.py:13
  65.0 2.2 %collective-permute-done.2 = f32[1,256,1,64]{1,3,2,0:T(8,128)S(1)} collective-permute-done((f32[1,256,1,64]{1,3,2,0:T(8,128)S(1)}, f32[1,256,1,64]{1,3,2,0:T(8,128)S(1)}, u32[]{:S(2)}, u32[]{:S(2)}) %collective-permute-start.2) | collective-permute-done | bytes 65568 | tf_op jit(solution)/shard_map/ppermute | solution.py:13
  67.2 0.1 fusion.4
  67.3 0.0 copy-done
  67.3 2.1 %fusion = bf16[1,256,4096]{2,1,0:T(8,128)(2,1)} fusion(bf16[256,192]{0,1:T(8,128)(2,1)S(1)} %fusion.4, bf16[192,4096]{1,0:T(8,128)(2,1)S(1)} %bitcast.44), kind=kOutput, calls=%fused_computation.1 | convolution fusion | flops 403701760 | bytes 3768320 | tf_op jit(solution)/shard_map/dot_general | solution.py:67
  (5 shorter events, 0.0 us)
Async XLA Ops:
  6.5 53.1 %all-gather.2.cloned.1.call-start = ((), (), s32[]{:S(2)}) async-start(), calls=%async_computation | async-start | bytes 1769472 | tf_op jit(solution)/shard_map/all_gather | solution.py:47
  7.4 4.9 %collective-permute-start.1 = (bf16[1,8,4096]{2,1,0:T(8,128)(2,1)S(1)}, bf16[1,8,4096]{2,1,0:T(8,128)(2,1)S(1)}, u32[]{:S(2)}, u32[]{:S(2)}) collective-permute-start(bf16[1,8,4096]{2,1,0:T(8,128)(2,1)S(1)} %get-tuple-element.6), channel_id=1, source_target_pairs={{8,0},{16,8},{24,16},{0,24},{9,1},{17,9},{25,17},{1,25},{10,2},{18... | collective-permute-start | bytes 196616 | tf_op jit(solution)/shard_map/ppermute | solution.py:13
  9.8 3.7 %collective-permute-start = (bf16[1,8,4096]{2,1,0:T(8,128)(2,1)S(1)}, bf16[1,8,4096]{2,1,0:T(8,128)(2,1)S(1)}, u32[]{:S(2)}, u32[]{:S(2)}) collective-permute-start(bf16[1,8,4096]{2,1,0:T(8,128)(2,1)S(1)} %get-tuple-element.6), channel_id=1, source_target_pairs={{24,0},{0,8},{8,16},{16,24},{25,1},{1,9},{9,17},{17,25},{26,2},{2,... | collective-permute-start | bytes 196616 | tf_op jit(solution)/shard_map/ppermute | solution.py:13
  14.3 27.8 %collective-permute-start.4 = (bf16[1]{0:T(256)(128)(2,1)}, bf16[1]{0:T(256)(128)(2,1)}, u32[]{:S(2)}, u32[]{:S(2)}) collective-permute-start(bf16[1]{0:T(256)(128)(2,1)} %param.4), channel_id=1, source_target_pairs={{24,0},{0,8},{8,16},{16,24},{25,1},{1,9},{9,17},{17,25},{26,2},{2,... | collective-permute-start | bytes 14 | tf_op jit(solution)/shard_map/ppermute | solution.py:13
  14.3 27.7 %collective-permute-start.5 = (bf16[1]{0:T(256)(128)(2,1)}, bf16[1]{0:T(256)(128)(2,1)}, u32[]{:S(2)}, u32[]{:S(2)}) collective-permute-start(bf16[1]{0:T(256)(128)(2,1)} %param.4), channel_id=1, source_target_pairs={{8,0},{16,8},{24,16},{0,24},{9,1},{17,9},{25,17},{1,25},{10,2},{18... | collective-permute-start | bytes 14 | tf_op jit(solution)/shard_map/ppermute | solution.py:13
  59.7 7.7 %copy-start = (bf16[3,1,64,4096]{3,2,1,0:T(8,128)(2,1)S(1)}, bf16[3,1,64,4096]{3,2,1,0:T(8,128)(2,1)}, u32[]{:S(2)}) copy-start(bf16[3,1,64,4096]{3,2,1,0:T(8,128)(2,1)} %all-gather.2.cloned.1.call-done) | copy-start | bytes 4718596
  62.7 2.3 %collective-permute-start.3 = (f32[1,256,1,64]{1,3,2,0:T(8,128)S(1)}, f32[1,256,1,64]{1,3,2,0:T(8,128)S(1)}, u32[]{:S(2)}, u32[]{:S(2)}) collective-permute-start(f32[1,256,1,64]{1,3,2,0:T(8,128)S(1)} %slice_bitcast_fusion), channel_id=1, source_target_pairs={{8,0},{16,8},{24,16},{0,24},{9,1},{17,9},{25,17},{1,25},{10,2},{18... | collective-permute-start | bytes 196616 | tf_op jit(solution)/shard_map/ppermute | solution.py:13
  63.1 4.1 %collective-permute-start.2 = (f32[1,256,1,64]{1,3,2,0:T(8,128)S(1)}, f32[1,256,1,64]{1,3,2,0:T(8,128)S(1)}, u32[]{:S(2)}, u32[]{:S(2)}) collective-permute-start(f32[1,256,1,64]{1,3,2,0:T(8,128)S(1)} %get-tuple-element.7), channel_id=1, source_target_pairs={{24,0},{0,8},{8,16},{16,24},{25,1},{1,9},{9,17},{17,25},{26,2},{2,... | collective-permute-start | bytes 196616 | tf_op jit(solution)/shard_map/ppermute | solution.py:13
Sparse Core Ops, SparseCore 0:
  14.4 45.2 all-gather.1
where the time goes:
time: 76.5 us; the launch traced here: 76.2 us
  waiting for transfers between devices  23.6 us (31%)
  blocking collectives  21.7 us (28%)
  between operations  14.8 us (19%)
  matrix products  5.09 us (7%)
  starting transfers between devices  4.87 us (6%)
  local copies, waits for them, and re-layouts  3.2 us (4%)
  other arithmetic  2.94 us (4%)
    unnamed x1, blocking collectives  21.7 us
    all_gather x1, waiting for transfers between devices, shards(): lax.all_gather(stacked, 'vir', axis=2, tiled=True)  16.2 us
    ppermute x6, waiting for transfers between devices, shifted_2(): return lax.ppermute(block, axis, route)  7.36 us
    ppermute x6, starting transfers between devices, shifted_2(): return lax.ppermute(block, axis, route)  4.87 us
    dot_general x1, matrix products, shards(): jnp.einsum('rp,cp->rc', resident, row_sets.reshape(block_count * occ_dev...  3.03 us
    unnamed x5, local copies, waits for them, and re-layouts  2.17 us
    dot_general x1, matrix products, shards(): jnp.dot(amplitude.reshape(occ_dev * vir_dev, block_count * occ_dev * batc...  2.06 us
  transfers between devices with their start and end apart: 7, of which 5 were waited for; matrix products, arithmetic and copies ran while one was open for 6% of the time, Pallas kernels for 0%

commit v1 on v0

v1 whole, which is shorter than its diff:
```python
import functools

import jax
import jax.numpy as jnp
from jax import lax
from jax.experimental import pallas as pl
from jax.experimental.pallas import tpu as pltpu
from jax.sharding import PartitionSpec as P

BATCH_DEV = 8
MESH = pl.DeviceIdType.MESH


def kernel(n_occ, n_vir, orb, ev_ref, eo_ref, out, a, head, raw, rows, mir_out, mir_in, outb,
           send_sem, recv_sem, local_sem, out_sem):
    f32, bf16 = jnp.float32, jnp.bfloat16
    nz = n_vir // 2
    aux = orb.shape[1]
    half = aux // 2
    cut = half // 2
    b = BATCH_DEV
    block = n_vir * b
    o, v = lax.axis_index("occ"), lax.axis_index("vir")
    z, x, core = v // 2, v % 2, o % 2
    along_x = (o, z * 2 + (1 - x))
    sibling = (o + 1 - 2 * core, v)
    far = ((o - 1 + 2 * core + n_occ) % n_occ, v)

    def along_z(s):
        return (o, ((z - s + nz) % nz) * 2 + x)

    barrier = pltpu.get_barrier_semaphore()
    for dev in [along_x, sibling, far] + [along_z(s) for s in range(1, nz)]:
        pl.semaphore_signal(barrier, inc=1, device_id=dev, device_id_type=MESH)

    get_head = pltpu.make_async_copy(orb.at[pl.ds(0, 16)], head, local_sem.at[0])
    get_a = pltpu.make_async_copy(orb, a, local_sem.at[1])
    get_head.start()
    get_a.start()
    get_head.wait()

    top = head[...].astype(f32)[0:b]
    raw[0, 0, 0, :, 0:half] = jnp.concatenate([top[:, :half], top[:, half:]], axis=0).astype(bf16)
    ev = ev_ref[...].astype(f32)
    lane = lax.broadcasted_iota(jnp.int32, (b, 128), 1)
    row = lax.broadcasted_iota(jnp.int32, (b, 128), 0)
    picked = jnp.where(lane == row, jnp.broadcast_to(ev[:, :128], (b, 128)), 0.0)
    batch_energy = jnp.broadcast_to(jnp.sum(picked, axis=1, keepdims=True), (b, 128))
    occ_energy = jnp.broadcast_to(eo_ref[...].astype(f32), (b, 128))
    raw[0, 0, 0, :, half:] = jnp.concatenate([batch_energy, occ_energy], axis=0).astype(bf16)

    def copy(kind, s, src, dst, dev):
        at = kind * nz + s
        return pltpu.make_async_remote_copy(
            src_ref=src, dst_ref=dst, send_sem=send_sem.at[at], recv_sem=recv_sem.at[at],
            device_id=dev, device_id_type=MESH)

    first, last = pl.ds(0, cut), pl.ds(cut, half + 128 - cut)
    to_z = [None] + [copy(0, s, raw.at[0, 0, 0], raw.at[0, s, 0], along_z(s)) for s in range(1, nz)]
    to_x = [copy(1, s, raw.at[0, s, 0], raw.at[0, s, 1], along_x) for s in range(nz)]
    to_far = [copy(2, s, raw.at[0, s, 0], raw.at[2, s, 0], far) for s in range(nz)]
    to_far_x = [copy(3, s, raw.at[0, s, 1, :, first], raw.at[2, s, 1, :, first], far) for s in range(nz)]
    far_to_x = [copy(4, s, raw.at[2, s, 0, :, last], raw.at[2, s, 1, :, last], along_x) for s in range(nz)]
    to_sib = [copy(5, s, raw.at[0, s, 0], raw.at[1, s, 0], sibling) for s in range(nz)]
    to_sib_x = [copy(6, s, raw.at[0, s, 1], raw.at[1, s, 1], sibling) for s in range(nz)]
    mirrors = [copy(7, q, mir_out.at[q], mir_in.at[q], dev) for q, dev in enumerate((sibling, far))]

    def unpack(q, s):
        p0 = raw[q, s, 0, :, 0:half].astype(f32)
        p1 = raw[q, s, 1, :, 0:half].astype(f32)
        at = pl.ds(q * block + s * 2 * b, 2 * b)
        rows[at, 0:half] = jnp.concatenate([p0[0:b], p1[0:b]], axis=0).astype(bf16)
        rows[at, half:] = jnp.concatenate([p0[b:], p1[b:]], axis=0).astype(bf16)

    pl.semaphore_wait(barrier, nz + 2)
    to_x[0].start()
    to_far[0].start()
    for s in range(1, nz):
        to_z[s].start()
    to_sib[0].start()
    for s in range(nz):
        if s + 1 < nz:
            to_z[s + 1].wait_recv()
            to_x[s + 1].start()
            to_far[s + 1].start()
            to_sib[s + 1].start()
        to_x[s].wait_recv()
        to_far_x[s].start()
        to_sib_x[s].start()
        to_far[s].wait_recv()
        far_to_x[s].start()
        unpack(0, s)
    get_a.wait()
    for s in range(nz):
        to_sib[s].wait_recv()
        to_sib_x[s].wait_recv()
        unpack(1, s)
    for s in range(nz):
        to_far_x[s].wait_recv()
        far_to_x[s].wait_recv()
        unpack(2, s)

    def coulomb_of(start, size):
        return lax.dot_general(rows[pl.ds(start, size), :], a[...], (((1,), (1,)), ((), ())),
                               preferred_element_type=f32)

    others = coulomb_of(block, 2 * block)
    for q in range(2):
        mir_out[q] = others[q * block:(q + 1) * block].astype(bf16)
        mirrors[q].start()
    own = coulomb_of(0, block)

    levels = jnp.concatenate([raw[0, s, t, :, half:].astype(f32)[0:b] for s in range(nz) for t in range(2)], axis=0)
    width = a.shape[0]
    reps = width // 128
    levels = jnp.concatenate([levels] * reps, axis=1)
    own_occ = raw[0, 0, 0, :, half:].astype(f32)[b:b + 1]
    base = ev + levels - jnp.concatenate([own_occ] * reps, axis=1)

    def amplitude_of(q, numerator):
        occ = raw[q, 0, 0, :, half:].astype(f32)[b:b + 1]
        return (numerator / (base - jnp.concatenate([occ] * reps, axis=1))).astype(bf16)

    parts = [amplitude_of(0, 2.0 * own - own)]
    for q in range(2):
        mirrors[q].wait_recv()
        parts.append(amplitude_of(q + 1, 2.0 * others[q * block:(q + 1) * block] - mir_in[q].astype(f32)))
    amplitude = jnp.concatenate(parts, axis=0).T

    chunk = outb.shape[2]
    for c in range(aux // chunk):
        at = pl.ds(c * chunk, chunk)
        outb[c] = jnp.dot(amplitude, rows[:, at], preferred_element_type=f32).astype(bf16)
        pltpu.make_async_copy(outb.at[c], out.at[:, at], out_sem.at[c]).start()
    for c in range(aux // chunk):
        pltpu.make_async_copy(outb.at[c], out.at[:, pl.ds(c * chunk, chunk)], out_sem.at[c]).wait()
    for sent in to_z[1:] + to_x + to_far + to_far_x + far_to_x + to_sib + to_sib_x + mirrors:
        sent.wait_send()


def shards(n_occ, n_vir, orbitals, eps_occ, eps_vir):
    occ_dev, vir_dev, aux = orbitals.shape
    nz = n_vir // 2
    block = n_vir * BATCH_DEV
    chunk = 512
    bf16 = jnp.bfloat16
    count = 7 * nz + 2
    density = pl.pallas_call(
        functools.partial(kernel, n_occ, n_vir),
        out_shape=jax.ShapeDtypeStruct((vir_dev, aux), bf16),
        in_specs=[pl.BlockSpec(memory_space=pl.ANY), pl.BlockSpec(memory_space=pltpu.VMEM),
                  pl.BlockSpec(memory_space=pltpu.VMEM)],
        out_specs=pl.BlockSpec(memory_space=pl.ANY),
        scratch_shapes=[
            pltpu.VMEM((vir_dev, aux), bf16),
            pltpu.VMEM((16, aux), bf16),
            pltpu.VMEM((3, nz, 2, 16, aux // 2 + 128), bf16),
            pltpu.VMEM((3 * block, aux), bf16),
            pltpu.VMEM((2, block, vir_dev), bf16),
            pltpu.VMEM((2, block, vir_dev), bf16),
            pltpu.VMEM((aux // chunk, vir_dev, chunk), bf16),
            pltpu.SemaphoreType.DMA((count,)),
            pltpu.SemaphoreType.DMA((count,)),
            pltpu.SemaphoreType.DMA((2,)),
            pltpu.SemaphoreType.DMA((aux // chunk,)),
        ],
        compiler_params=pltpu.CompilerParams(
            collective_id=0, has_side_effects=True, vmem_limit_bytes=48 * 1024 * 1024),
        name="density",
    )(orbitals.reshape(vir_dev, aux), eps_vir.reshape(1, -1), eps_occ.reshape(1, 1))
    return density.reshape(occ_dev, vir_dev, aux)


def solution(mesh):
    return jax.shard_map(
        functools.partial(shards, mesh.shape["occ"], mesh.shape["vir"]),
        mesh=mesh,
        in_specs=(P("occ", "vir", None), P("occ"), P("vir")),
        out_specs=P("occ", "vir", None),
        check_vma=False,
    )
```

time: 76.5 us -> 32 us (0.42)
  the two profiles are of different devices: /device:TPU:0 before, /device:TPU:9 now
where the time goes in v1:
time: 32 us; the launch traced here: 31.8 us
  Pallas kernels  27.6 us (86%)
  local copies, waits for them, and re-layouts  3.57 us (11%)
  between operations  0.67 us (2%)
    pallas_call x1, Pallas kernels, shards(): pl.pallas_call(functools.partial(kernel, n_occ, n_vir), out_shape=jax.Sha...  27.6 us
    unnamed x3, local copies, waits for them, and re-layouts  2.91 us
    reshape x1, local copies, waits for them, and re-layouts, shards(): eps_vir.reshape(1, -1)  0.66 us

profile of v1, /device:TPU:9, one launch (start us, length us, event | category | flops | bytes accessed | tf_op | source)
XLA Modules:
  0.0 31.8 jit_solution(8230924963633383329)
XLA Ops:
  0.7 0.7 %reshape.13.ev_ref = bf16[1,256]{1,0:T(2,128)(2,1)S(1)} reshape(bf16[256]{0:T(256)(128)(2,1)} %param.5) | data formatting | bytes 1024 | tf_op jit(solution)/shard_map/reshape | solution.py:170
  1.3 0.0 copy-start
  1.3 1.6 %copy-done = bf16[1,256,4096]{2,1,0:T(8,128)(2,1)S(1)} copy-done((bf16[1,256,4096]{2,1,0:T(8,128)(2,1)S(1)}, bf16[1,256,4096]{2,1,0:T(8,128)(2,1)}, u32[]{:S(2)}) %copy-start) | copy-done | bytes 2097176
  2.9 27.6 %density.1 = bf16[256,4096]{1,0:T(8,128)(2,1)S(1)} custom-call(bf16[256,4096]{1,0:T(8,128)(2,1)S(1)} %bitcast.5, bf16[1,256]{1,0:T(2,128)(2,1)S(1)} %reshape.13.ev_ref, bf16[1,1]{1,0:T(2,128)(2,1)} %bitcast.3.eo_ref), custom_call_target="tpu_custom_call" | custom-call | tf_op jit(solution)/shard_map/density/pallas_call | solution.py:148
  30.5 1.3 %copy.6 = bf16[1,256,4096]{2,1,0:T(8,128)(2,1)} copy(bf16[1,256,4096]{2,1,0:T(8,128)(2,1)S(1)} %bitcast.4) | data formatting | bytes 4194304
Async XLA Ops:
  1.3 1.6 %copy-start = (bf16[1,256,4096]{2,1,0:T(8,128)(2,1)S(1)}, bf16[1,256,4096]{2,1,0:T(8,128)(2,1)}, u32[]{:S(2)}) copy-start(bf16[1,256,4096]{2,1,0:T(8,128)(2,1)} %param.3) | copy-start | bytes 6291460

commit v2 on v1

v2 whole, which is shorter than its diff:
```python
import functools

import jax
import jax.numpy as jnp
from jax import lax
from jax.experimental import pallas as pl
from jax.experimental.pallas import tpu as pltpu
from jax.sharding import PartitionSpec as P

BATCH_DEV = 8
MESH = pl.DeviceIdType.MESH


def kernel(n_occ, n_vir, orb, ev_ref, eo_ref, out, a, head, raw, rows, mir_out, mir_in,
           send_sem, recv_sem, local_sem):
    f32, bf16 = jnp.float32, jnp.bfloat16
    nz = n_vir // 2
    aux = orb.shape[1]
    half = aux // 2
    cut = half // 2
    b = BATCH_DEV
    block = n_vir * b
    o, v = lax.axis_index("occ"), lax.axis_index("vir")
    z, x, core = v // 2, v % 2, o % 2
    along_x = (o, z * 2 + (1 - x))
    sibling = (o + 1 - 2 * core, v)
    far = ((o - 1 + 2 * core + n_occ) % n_occ, v)
    has_up, has_down = z < nz - 1, z > 0
    up, down = (o, v + 2), (o, v - 2)

    inner = jnp.minimum(z, nz - 1 - z)
    order = []
    for k in range(nz):
        near = z - (k + 1) // 2 if k % 2 else z + k // 2
        order.append(jnp.where(k <= 2 * inner, near, jnp.where(2 * z <= nz - 1, k, nz - 1 - k)))

    barrier = pltpu.get_barrier_semaphore()
    for dev in (along_x, sibling, far):
        pl.semaphore_signal(barrier, inc=1, device_id=dev, device_id_type=MESH)

    @pl.when(has_up)
    def _():
        pl.semaphore_signal(barrier, inc=1, device_id=up, device_id_type=MESH)

    @pl.when(has_down)
    def _():
        pl.semaphore_signal(barrier, inc=1, device_id=down, device_id_type=MESH)

    get_head = pltpu.make_async_copy(orb.at[pl.ds(0, 16)], head, local_sem.at[0])
    get_a = pltpu.make_async_copy(orb, a, local_sem.at[1])
    get_head.start()
    get_a.start()
    get_head.wait()

    top = head[...].astype(f32)[0:b]
    raw[0, z, 0, :, 0:half] = jnp.concatenate([top[:, :half], top[:, half:]], axis=0).astype(bf16)
    ev = ev_ref[...].reshape(1, -1).astype(f32)
    lane = lax.broadcasted_iota(jnp.int32, (b, 128), 1)
    row = lax.broadcasted_iota(jnp.int32, (b, 128), 0)
    picked = jnp.where(lane == row, jnp.broadcast_to(ev[:, :128], (b, 128)), 0.0)
    batch_energy = jnp.broadcast_to(jnp.sum(picked, axis=1, keepdims=True), (b, 128))
    occ_energy = jnp.broadcast_to(eo_ref[...].reshape(1, 1).astype(f32), (b, 128))
    raw[0, z, 0, :, half:] = jnp.concatenate([batch_energy, occ_energy], axis=0).astype(bf16)

    parts = (pl.ds(0, cut), pl.ds(cut, half + 128 - cut))

    def copy(kind, s, src, dst, dev, send_kind=None):
        send_kind = kind if send_kind is None else send_kind
        return pltpu.make_async_remote_copy(
            src_ref=src, dst_ref=dst, send_sem=send_sem.at[send_kind, s], recv_sem=recv_sem.at[kind, s],
            device_id=dev, device_id_type=MESH)

    def on_z(s, h, dev, send_kind=None):
        piece = raw.at[0, s, 0, :, parts[h]]
        return copy(h, s, piece, piece, dev, send_kind)

    def on_x(s, h):
        return copy(2 + h, s, raw.at[0, s, 0, :, parts[h]], raw.at[0, s, 1, :, parts[h]], along_x)

    def on_far(s, h):
        return copy(4 + h, s, raw.at[0, s, 0, :, parts[h]], raw.at[2, s, 0, :, parts[h]], far)

    def x_to_far(s):
        return copy(6, s, raw.at[0, s, 1, :, parts[0]], raw.at[2, s, 1, :, parts[0]], far)

    def far_to_x(s):
        return copy(7, s, raw.at[2, s, 0, :, parts[1]], raw.at[2, s, 1, :, parts[1]], along_x)

    def on_sib(s, t):
        return copy(8 + t, s, raw.at[0, s, t], raw.at[1, s, t], sibling)

    early = (nz - 1) * 2 * b

    def mirror(q):
        if q == 0:
            return copy(10, 0, mir_out.at[pl.ds(0, block)], mir_in.at[pl.ds(0, block)], sibling)
        at = pl.ds(block, early) if q == 1 else pl.ds(block + early, block - early)
        return copy(10, q, mir_out.at[at], mir_in.at[at], far)

    def relay(s, h, then):
        @pl.when(jnp.logical_and(s < z, has_up))
        def _():
            then(on_z(s, h, up))

        @pl.when(jnp.logical_and(s > z, has_down))
        def _():
            then(on_z(s, h, down))

    def own_z(h, then):
        @pl.when(has_up)
        def _():
            then(on_z(z, h, up))

        @pl.when(has_down)
        def _():
            then(on_z(z, h, down, 11 + h))

    def unpack(q, k):
        s = order[k]
        p0 = raw[q, s, 0, :, 0:half].astype(f32)
        p1 = raw[q, s, 1, :, 0:half].astype(f32)
        at = pl.ds(q * block + k * 2 * b, 2 * b)
        rows[at, 0:half] = jnp.concatenate([p0[0:b], p1[0:b]], axis=0).astype(bf16)
        rows[at, half:] = jnp.concatenate([p0[b:], p1[b:]], axis=0).astype(bf16)

    pl.semaphore_wait(barrier, 3 + jnp.where(has_up, 1, 0) + jnp.where(has_down, 1, 0))

    def start(c):
        c.start()

    own_z(0, start)
    on_x(z, 0).start()
    on_far(z, 1).start()
    own_z(1, start)
    on_x(z, 1).start()
    on_far(z, 0).start()
    on_sib(z, 0).start()
    for k in range(nz):
        s = order[k]
        if k + 1 < nz:
            following = order[k + 1]
            for h in range(2):
                on_z(following, h, up).wait_recv()
                relay(following, h, start)
                on_x(following, h).start()
                on_far(following, h).start()
            on_sib(following, 0).start()
        on_x(s, 0).wait_recv()
        x_to_far(s).start()
        on_far(s, 1).wait_recv()
        far_to_x(s).start()
        on_x(s, 1).wait_recv()
        on_sib(s, 1).start()
        unpack(0, k)
    get_a.wait()

    def wait_far(k):
        on_far(order[k], 0).wait_recv()
        x_to_far(order[k]).wait_recv()
        far_to_x(order[k]).wait_recv()
        unpack(2, k)

    def coulomb_of(start, size):
        return lax.dot_general(rows[pl.ds(start, size), :], a[...], (((1,), (1,)), ((), ())),
                               preferred_element_type=f32)

    for k in range(nz - 1):
        wait_far(k)
    far_early = coulomb_of(2 * block, early)
    mir_out[pl.ds(block, early), :] = far_early.astype(bf16)
    mirror(1).start()
    for k in range(nz):
        on_sib(order[k], 0).wait_recv()
        on_sib(order[k], 1).wait_recv()
        unpack(1, k)
    near = coulomb_of(0, 2 * block)
    mir_out[pl.ds(0, block), :] = near[block:].astype(bf16)
    mirror(0).start()
    wait_far(nz - 1)
    far_late = coulomb_of(2 * block + early, block - early)
    mir_out[pl.ds(block + early, block - early), :] = far_late.astype(bf16)
    mirror(2).start()

    levels = jnp.concatenate([raw[0, order[k], t, :, half:].astype(f32)[0:b] for k in range(nz) for t in range(2)], axis=0)
    width = a.shape[0]
    reps = width // 128
    levels = jnp.concatenate([levels] * reps, axis=1)

    def occ_of(q):
        return jnp.concatenate([raw[q, z, 0, :, half:].astype(f32)[b:b + 1]] * reps, axis=1)

    base = ev + levels - occ_of(0)
    amp_own = ((2.0 * near[:block] - near[:block]) / (base - occ_of(0))).astype(bf16)
    mirror(0).wait_recv()
    amp_sib = ((2.0 * near[block:] - mir_in[pl.ds(0, block), :].astype(f32)) / (base - occ_of(1))).astype(bf16)
    mirror(1).wait_recv()
    mirror(2).wait_recv()
    far_all = jnp.concatenate([far_early, far_late], axis=0)
    amp_far = ((2.0 * far_all - mir_in[pl.ds(block, block), :].astype(f32)) / (base - occ_of(2))).astype(bf16)
    amplitude = jnp.concatenate([amp_own, amp_sib, amp_far], axis=0).T

    chunk = 512
    for c in range(aux // chunk):
        at = pl.ds(c * chunk, chunk)
        out[:, at] = jnp.dot(amplitude, rows[:, at], preferred_element_type=f32).astype(bf16)

    def finish(c):
        c.wait_send()

    for h in range(2):
        own_z(h, finish)
    for k in range(nz):
        s = order[k]
        for h in range(2):
            if k:
                relay(s, h, finish)
            on_x(s, h).wait_send()
            on_far(s, h).wait_send()
            on_sib(s, h).wait_send()
        x_to_far(s).wait_send()
        far_to_x(s).wait_send()
    for q in range(3):
        mirror(q).wait_send()


def shards(n_occ, n_vir, orbitals, eps_occ, eps_vir):
    occ_dev, vir_dev, aux = orbitals.shape
    nz = n_vir // 2
    block = n_vir * BATCH_DEV
    bf16 = jnp.bfloat16
    density = pl.pallas_call(
        functools.partial(kernel, n_occ, n_vir),
        out_shape=jax.ShapeDtypeStruct((vir_dev, aux), bf16),
        in_specs=[pl.BlockSpec(memory_space=pltpu.HBM), pl.BlockSpec(memory_space=pltpu.VMEM),
                  pl.BlockSpec(memory_space=pltpu.VMEM)],
        out_specs=pl.BlockSpec(memory_space=pltpu.VMEM),
        scratch_shapes=[
            pltpu.VMEM((vir_dev, aux), bf16),
            pltpu.VMEM((16, aux), bf16),
            pltpu.VMEM((3, nz, 2, 16, aux // 2 + 128), bf16),
            pltpu.VMEM((3 * block, aux), bf16),
            pltpu.VMEM((2 * block, vir_dev), bf16),
            pltpu.VMEM((2 * block, vir_dev), bf16),
            pltpu.SemaphoreType.DMA((13, nz)),
            pltpu.SemaphoreType.DMA((11, nz)),
            pltpu.SemaphoreType.DMA((2,)),
        ],
        compiler_params=pltpu.CompilerParams(
            collective_id=0, has_side_effects=True, vmem_limit_bytes=48 * 1024 * 1024),
        name="density",
    )(orbitals.reshape(vir_dev, aux), eps_vir, eps_occ)
    return density.reshape(occ_dev, vir_dev, aux)


def solution(mesh):
    return jax.shard_map(
        functools.partial(shards, mesh.shape["occ"], mesh.shape["vir"]),
        mesh=mesh,
        in_specs=(P("occ", "vir", None), P("occ"), P("vir")),
        out_specs=P("occ", "vir", None),
        check_vma=False,
    )
```

time: 32 us -> 30.3 us (0.947)
  the two profiles are of different devices: /device:TPU:9 before, /device:TPU:0 now
where the time goes in v2:
time: 30.3 us; the launch traced here: 30 us
  Pallas kernels  25.7 us (85%)
  local copies, waits for them, and re-layouts  3.56 us (12%)
  between operations  0.68 us (2%)
    pallas_call x1, Pallas kernels, shards(): pl.pallas_call(functools.partial(kernel, n_occ, n_vir), out_shape=jax.Sha...  25.7 us
    unnamed x5, local copies, waits for them, and re-layouts  3.56 us

profile of v2, /device:TPU:0, one launch (start us, length us, event | category | flops | bytes accessed | tf_op | source)
XLA Modules:
  0.0 30.0 jit_solution(7869946530907678619)
XLA Ops:
  0.7 0.0 copy-start
  0.7 1.6 %copy-done = bf16[1,256,4096]{2,1,0:T(8,128)(2,1)S(1)} copy-done((bf16[1,256,4096]{2,1,0:T(8,128)(2,1)S(1)}, bf16[1,256,4096]{2,1,0:T(8,128)(2,1)}, u32[]{:S(2)}) %copy-start) | copy-done | bytes 2097176
  2.3 0.0 copy-start.1
  2.3 0.7 %copy-done.1 = bf16[256]{0:T(256)(128)(2,1)S(1)} copy-done((bf16[256]{0:T(256)(128)(2,1)S(1)}, bf16[256]{0:T(256)(128)(2,1)}, u32[]{:S(2)}) %copy-start.1) | copy-done | bytes 536
  2.9 25.7 %density.1 = bf16[256,4096]{1,0:T(8,128)(2,1)S(1)} custom-call(bf16[256,4096]{1,0:T(8,128)(2,1)S(1)} %bitcast.3, bf16[256]{0:T(256)(128)(2,1)S(1)} %copy-done.1, bf16[1]{0:T(256)(128)(2,1)S(6)} %copy.5.eo_ref), custom_call_target="tpu_custom_call" | custom-call | tf_op jit(solution)/shard_map/density/pallas_call | solution.py:231
  28.6 1.3 %copy.6 = bf16[1,256,4096]{2,1,0:T(8,128)(2,1)} copy(bf16[1,256,4096]{2,1,0:T(8,128)(2,1)S(1)} %bitcast.2) | data formatting | bytes 4194304
Async XLA Ops:
  0.7 1.6 %copy-start = (bf16[1,256,4096]{2,1,0:T(8,128)(2,1)S(1)}, bf16[1,256,4096]{2,1,0:T(8,128)(2,1)}, u32[]{:S(2)}) copy-start(bf16[1,256,4096]{2,1,0:T(8,128)(2,1)} %param.3) | copy-start | bytes 6291460
  2.3 0.7 %copy-start.1 = (bf16[256]{0:T(256)(128)(2,1)S(1)}, bf16[256]{0:T(256)(128)(2,1)}, u32[]{:S(2)}) copy-start(bf16[256]{0:T(256)(128)(2,1)} %ev_ref.1) | copy-start | bytes 1540

commit v3 on v2

--- a/solution.py
+++ b/solution.py
@@ -11,7 +11,7 @@
 MESH = pl.DeviceIdType.MESH
 
 
-def kernel(n_occ, n_vir, orb, ev_ref, eo_ref, out, a, head, raw, rows, mir_out, mir_in,
+def kernel(n_occ, n_vir, orb, ev_hbm, eo_ref, amp_ref, rows, a, head, ev_ref, raw, mir_out, mir_in,
            send_sem, recv_sem, local_sem):
     f32, bf16 = jnp.float32, jnp.bfloat16
     nz = n_vir // 2
@@ -25,9 +25,6 @@
     along_x = (o, z * 2 + (1 - x))
     sibling = (o + 1 - 2 * core, v)
     far = ((o - 1 + 2 * core + n_occ) % n_occ, v)
-    has_up, has_down = z < nz - 1, z > 0
-    up, down = (o, v + 2), (o, v - 2)
-
     inner = jnp.minimum(z, nz - 1 - z)
     order = []
     for k in range(nz):
@@ -35,22 +32,17 @@
         order.append(jnp.where(k <= 2 * inner, near, jnp.where(2 * z <= nz - 1, k, nz - 1 - k)))
 
     barrier = pltpu.get_barrier_semaphore()
-    for dev in (along_x, sibling, far):
+    for dev in [along_x, sibling, far] + [(o, s * 2 + x) for s in order[1:]]:
         pl.semaphore_signal(barrier, inc=1, device_id=dev, device_id_type=MESH)
-
-    @pl.when(has_up)
-    def _():
-        pl.semaphore_signal(barrier, inc=1, device_id=up, device_id_type=MESH)
-
-    @pl.when(has_down)
-    def _():
-        pl.semaphore_signal(barrier, inc=1, device_id=down, device_id_type=MESH)
 
     get_head = pltpu.make_async_copy(orb.at[pl.ds(0, 16)], head, local_sem.at[0])
     get_a = pltpu.make_async_copy(orb, a, local_sem.at[1])
+    get_ev = pltpu.make_async_copy(ev_hbm, ev_ref, local_sem.at[2])
     get_head.start()
+    get_ev.start()
     get_a.start()
     get_head.wait()
+    get_ev.wait()
 
     top = head[...].astype(f32)[0:b]
     raw[0, z, 0, :, 0:half] = jnp.concatenate([top[:, :half], top[:, half:]], axis=0).astype(bf16)
@@ -64,15 +56,18 @@
 
     parts = (pl.ds(0, cut), pl.ds(cut, half + 128 - cut))
 
-    def copy(kind, s, src, dst, dev, send_kind=None):
-        send_kind = kind if send_kind is None else send_kind
+    def copy(kind, s, src, dst, dev, send_at=None):
         return pltpu.make_async_remote_copy(
-            src_ref=src, dst_ref=dst, send_sem=send_sem.at[send_kind, s], recv_sem=recv_sem.at[kind, s],
-            device_id=dev, device_id_type=MESH)
-
-    def on_z(s, h, dev, send_kind=None):
+            src_ref=src, dst_ref=dst, send_sem=send_sem.at[kind, s if send_at is None else send_at],
+            recv_sem=recv_sem.at[kind, s], device_id=dev, device_id_type=MESH)
+
+    def to_z(s, h):
+        piece = raw.at[0, z, 0, :, parts[h]]
+        return copy(h, z, piece, piece, (o, s * 2 + x), s)
+
+    def from_z(s, h):
         piece = raw.at[0, s, 0, :, parts[h]]
-        return copy(h, s, piece, piece, dev, send_kind)
+        return copy(h, s, piece, piece, (o, s * 2 + x))
 
     def on_x(s, h):
         return copy(2 + h, s, raw.at[0, s, 0, :, parts[h]], raw.at[0, s, 1, :, parts[h]], along_x)
@@ -96,24 +91,6 @@
             return copy(10, 0, mir_out.at[pl.ds(0, block)], mir_in.at[pl.ds(0, block)], sibling)
         at = pl.ds(block, early) if q == 1 else pl.ds(block + early, block - early)
         return copy(10, q, mir_out.at[at], mir_in.at[at], far)
-
-    def relay(s, h, then):
-        @pl.when(jnp.logical_and(s < z, has_up))
-        def _():
-            then(on_z(s, h, up))
-
-        @pl.when(jnp.logical_and(s > z, has_down))
-        def _():
-            then(on_z(s, h, down))
-
-    def own_z(h, then):
-        @pl.when(has_up)
-        def _():
-            then(on_z(z, h, up))
-
-        @pl.when(has_down)
-        def _():
-            then(on_z(z, h, down, 11 + h))
 
     def unpack(q, k):
         s = order[k]
@@ -123,25 +100,23 @@
         rows[at, 0:half] = jnp.concatenate([p0[0:b], p1[0:b]], axis=0).astype(bf16)
         rows[at, half:] = jnp.concatenate([p0[b:], p1[b:]], axis=0).astype(bf16)
 
-    pl.semaphore_wait(barrier, 3 + jnp.where(has_up, 1, 0) + jnp.where(has_down, 1, 0))
-
-    def start(c):
-        c.start()
-
-    own_z(0, start)
+    pl.semaphore_wait(barrier, nz + 2)
+    to_z(order[1], 0).start()
     on_x(z, 0).start()
     on_far(z, 1).start()
-    own_z(1, start)
+    to_z(order[1], 1).start()
     on_x(z, 1).start()
     on_far(z, 0).start()
+    for k in range(2, nz):
+        to_z(order[k], 0).start()
+        to_z(order[k], 1).start()
     on_sib(z, 0).start()
     for k in range(nz):
         s = order[k]
         if k + 1 < nz:
             following = order[k + 1]
             for h in range(2):
-                on_z(following, h, up).wait_recv()
-                relay(following, h, start)
+                from_z(following, h).wait_recv()
                 on_x(following, h).start()
                 on_far(following, h).start()
             on_sib(following, 0).start()
@@ -197,23 +172,13 @@
     mirror(2).wait_recv()
     far_all = jnp.concatenate([far_early, far_late], axis=0)
     amp_far = ((2.0 * far_all - mir_in[pl.ds(block, block), :].astype(f32)) / (base - occ_of(2))).astype(bf16)
-    amplitude = jnp.concatenate([amp_own, amp_sib, amp_far], axis=0).T
-
-    chunk = 512
-    for c in range(aux // chunk):
-        at = pl.ds(c * chunk, chunk)
-        out[:, at] = jnp.dot(amplitude, rows[:, at], preferred_element_type=f32).astype(bf16)
-
-    def finish(c):
-        c.wait_send()
-
-    for h in range(2):
-        own_z(h, finish)
+    amp_ref[...] = jnp.concatenate([amp_own, amp_sib, amp_far], axis=0).T
+
     for k in range(nz):
         s = order[k]
         for h in range(2):
             if k:
-                relay(s, h, finish)
+                to_z(s, h).wait_send()
             on_x(s, h).wait_send()
             on_far(s, h).wait_send()
             on_sib(s, h).wait_send()
@@ -228,27 +193,28 @@
     nz = n_vir // 2
     block = n_vir * BATCH_DEV
     bf16 = jnp.bfloat16
-    density = pl.pallas_call(
+    amplitude, rows = pl.pallas_call(
         functools.partial(kernel, n_occ, n_vir),
-        out_shape=jax.ShapeDtypeStruct((vir_dev, aux), bf16),
-        in_specs=[pl.BlockSpec(memory_space=pltpu.HBM), pl.BlockSpec(memory_space=pltpu.VMEM),
+        out_shape=(jax.ShapeDtypeStruct((vir_dev, 3 * block), bf16), jax.ShapeDtypeStruct((3 * block, aux), bf16)),
+        in_specs=[pl.BlockSpec(memory_space=pltpu.HBM), pl.BlockSpec(memory_space=pltpu.HBM),
                   pl.BlockSpec(memory_space=pltpu.VMEM)],
-        out_specs=pl.BlockSpec(memory_space=pltpu.VMEM),
+        out_specs=[pl.BlockSpec(memory_space=pltpu.VMEM)] * 2,
         scratch_shapes=[
             pltpu.VMEM((vir_dev, aux), bf16),
             pltpu.VMEM((16, aux), bf16),
+            pltpu.VMEM((vir_dev,), bf16),
             pltpu.VMEM((3, nz, 2, 16, aux // 2 + 128), bf16),
-            pltpu.VMEM((3 * block, aux), bf16),
             pltpu.VMEM((2 * block, vir_dev), bf16),
             pltpu.VMEM((2 * block, vir_dev), bf16),
-            pltpu.SemaphoreType.DMA((13, nz)),
             pltpu.SemaphoreType.DMA((11, nz)),
-            pltpu.SemaphoreType.DMA((2,)),
+            pltpu.SemaphoreType.DMA((11, nz)),
+            pltpu.SemaphoreType.DMA((3,)),
         ],
         compiler_params=pltpu.CompilerParams(
-            collective_id=0, has_side_effects=True, vmem_limit_bytes=48 * 1024 * 1024),
-        name="density",
+            collective_id=0, has_side_effects=True, vmem_limit_bytes=51 * 1024 * 1024),
+        name="amplitude",
     )(orbitals.reshape(vir_dev, aux), eps_vir, eps_occ)
+    density = jnp.dot(amplitude, rows, preferred_element_type=jnp.float32).astype(bf16)
     return density.reshape(occ_dev, vir_dev, aux)
 
 

time: 30.3 us -> 27.8 us (0.917)
  local copies, waits for them, and re-layouts: 3.56 us -> 0.65 us
  matrix products: 0 us -> 2.03 us
  Pallas kernels: 25.7 us -> 24.3 us
    unnamed x5 -> x2, local copies, waits for them, and re-layouts: 3.56 us -> 0.65 us
    dot_general x0 -> x1, matrix products: none -> 2.03 us  [shards(): jnp.dot(amplitude, rows, preferred_element_type=jnp.float32).astype(bf16)]
    pallas_call x1, Pallas kernels: 25.7 us -> 24.3 us  [shards(): pl.pallas_call(functools.partial(kernel, n_occ, n_vir), out_shape=(jax.Sh...]
where the time goes in v3:
time: 27.8 us; the launch traced here: 27.6 us
  Pallas kernels  24.3 us (87%)
  matrix products  2.03 us (7%)
  between operations  0.68 us (2%)
  local copies, waits for them, and re-layouts  0.65 us (2%)
    pallas_call x1, Pallas kernels, shards(): pl.pallas_call(functools.partial(kernel, n_occ, n_vir), out_shape=(jax.Sh...  24.3 us
    dot_general x1, matrix products, shards(): jnp.dot(amplitude, rows, preferred_element_type=jnp.float32).astype(bf16)  2.03 us
    unnamed x2, local copies, waits for them, and re-layouts  0.65 us

profile of v3, /device:TPU:0, one launch (start us, length us, event | category | flops | bytes accessed | tf_op | source)
XLA Modules:
  0.0 27.6 jit_solution(7678964595656519312)
XLA Ops:
  0.7 0.0 copy-start
  0.7 0.6 %copy-done = bf16[256]{0:T(256)(128)(2,1)S(1)} copy-done((bf16[256]{0:T(256)(128)(2,1)S(1)}, bf16[256]{0:T(256)(128)(2,1)}, u32[]{:S(2)}) %copy-start) | copy-done | bytes 536
  1.3 24.3 %amplitude.1 = (bf16[256,192]{1,0:T(8,128)(2,1)S(1)}, bf16[192,4096]{1,0:T(8,128)(2,1)S(1)}) custom-call(bf16[256,4096]{1,0:T(8,128)(2,1)} %bitcast.5, bf16[256]{0:T(256)(128)(2,1)S(1)} %copy-done, bf16[1]{0:T(256)(128)(2,1)S(6)} %copy.4.eo_ref), custom_call_target="tpu_custom_call" | custom-call | tf_op jit(solution)/shard_map/amplitude/pallas_call | solution.py:196
  25.6 2.0 %fusion = bf16[1,256,4096]{2,1,0:T(8,128)(2,1)} fusion(bf16[256,192]{1,0:T(8,128)(2,1)S(1)} %get-tuple-element.7, bf16[192,4096]{1,0:T(8,128)(2,1)S(1)} %get-tuple-element.8), kind=kOutput, calls=%fused_computation.1 | convolution fusion | flops 403701760 | bytes 3768320 | tf_op jit(solution)/shard_map/dot_general | solution.py:217
Async XLA Ops:
  0.7 0.7 %copy-start = (bf16[256]{0:T(256)(128)(2,1)S(1)}, bf16[256]{0:T(256)(128)(2,1)}, u32[]{:S(2)}) copy-start(bf16[256]{0:T(256)(128)(2,1)} %ev_hbm.1) | copy-start | bytes 1540
